TPU v7x, 512 devices: a whole 4x8x8 slice. The times are simulated.
512 devices in a mesh: angle: 16 (over y, core), tile: 32 (over x, z).
Axes of the slice: x: 4, y: 8, z: 8, core: 2. Of those that a mesh axis runs over, the one named last changes fastest.
Arguments:
- patches: bfloat16 [16, 256, 2, 128, 128], P('angle', 'tile'), may hold values from -6 to 6
- magnitudes: bfloat16 [16, 2048, 128, 128], P('angle', 'tile'), may hold values from 0.099609375 to 3
- probe: float32 [2, 128, 128], replicated, may hold values from -6 to 6
- owners: int32 [16, 256, 1], P('angle', 'tile'), may hold values from 0 to 31; in each aligned block of 8 rows (0 to 7, 8 to 15, ..., all dimensions but the last counted through in order) at most 2 rows name the same one
- scan_rows: int32 [16, 256], P('angle', 'tile'), may hold values from 0 to 384
- scan_cols: int32 [16, 256], P('angle', 'tile'), may hold values from 0 to 896
- slab_rows: int32 [32, 16], P('tile'), may hold values from 0 to 2, as said below
- angle_tan: float32 [16], replicated, may hold values from -0.4 to 0.4
- prior_in: bfloat16 [16, 1, 3, 3], replicated, may hold values from -2 to 2
- prior_out: bfloat16 [1, 16, 3, 3], replicated, may hold values from -0.5 to 0.5
Outputs:
- volume: float32 [32, 32, 16, 1024], P('tile', 'angle')
Inputs may be any that keep to these rules, and one draw needn't show every extreme that they name: `owners`: in the patches of one device, no owner is named by more than 2, and in some devices one owner is named exactly 2 times. Each row of slab_rows sums to 16, and in every row some slab has exactly 2 rows.
All inputs are finite; a program needn't handle non-finite values.
Results may differ from a plain program's by a relative error of at most 0.022.
Values may be sent and summed in bfloat16 or wider, within the bound.
A program may use at most 64 MiB of HBM per device.

v0:
```python
import math
import jax
import jax.numpy as jnp
from jax import lax
from jax.sharding import PartitionSpec as P

H = 512
W = 1024
XW = 16


def dft_table(side):
    index = jnp.arange(side, dtype=jnp.int32)
    product = index[:, None] * index[None, :] % side
    phase = product.astype(jnp.float32) * (2.0 * math.pi / side)
    scale = 1.0 / math.sqrt(side)
    real = jnp.cos(phase) * scale
    imag = -jnp.sin(phase) * scale
    upper = jnp.concatenate([real, imag], axis=1)
    lower = jnp.concatenate([-imag, real], axis=1)
    return jnp.concatenate([upper, lower], axis=0).astype(jnp.bfloat16)


def correct_all(waves, measured, table):
    number = waves.shape[0]
    side = waves.shape[2]
    left = table.T
    joined = jnp.concatenate([waves[:, 0], waves[:, 1]], axis=2).reshape(number * side, 2 * side)
    half = jnp.dot(joined, table, preferred_element_type=jnp.float32).astype(jnp.bfloat16)
    half = half.reshape(number, side, 2 * side)
    stacked = jnp.concatenate([half[:, :, :side], half[:, :, side:]], axis=1)
    stacked = jnp.transpose(stacked, (1, 0, 2)).reshape(2 * side, number * side)
    spectrum = jnp.dot(left, stacked, preferred_element_type=jnp.float32).reshape(
        2 * side, number, side
    )
    real_part = spectrum[:side]
    imag_part = spectrum[side:]
    level = jnp.transpose(measured, (1, 0, 2)).astype(jnp.float32)
    factor = level / jnp.sqrt(real_part * real_part + imag_part * imag_part + 0.25)
    target = jnp.concatenate([real_part * factor, imag_part * factor], axis=2).astype(jnp.bfloat16)
    back = jnp.dot(
        target.reshape(side * number, 2 * side), left, preferred_element_type=jnp.float32
    )
    back = back.astype(jnp.bfloat16).reshape(side, number, 2 * side)
    stacked_back = jnp.concatenate([back[:, :, :side], back[:, :, side:]], axis=0).reshape(
        2 * side, number * side
    )
    result = jnp.dot(table, stacked_back, preferred_element_type=jnp.float32).reshape(
        2, side, number, side
    )
    return jnp.transpose(result, (2, 0, 1, 3)).astype(jnp.bfloat16)


def backproject(sino, angle_tan, width):
    count = sino.shape[1]
    offsets = jnp.arange(XW, dtype=jnp.float32) - (XW - 1) / 2.0
    spread_cols = int(0.2 * (XW - 1)) + 2
    shifts = jnp.arange(-spread_cols, spread_cols + 1, dtype=jnp.int32).astype(jnp.float32)

    def add_angle(total, item):
        rows, tangent = item
        shifted = offsets * tangent
        floor_shift = jnp.floor(shifted)
        fraction = shifted - floor_shift
        low_hit = (shifts[None, :] == floor_shift[:, None]).astype(jnp.float32)
        high_hit = (shifts[None, :] == floor_shift[:, None] + 1.0).astype(jnp.float32)
        weights = (1.0 - fraction)[:, None] * low_hit + fraction[:, None] * high_hit
        padded = jnp.pad(rows, ((0, 0), (spread_cols, spread_cols)))
        columns_stack = jnp.stack(
            [padded[:, step : step + width] for step in range(2 * spread_cols + 1)], axis=0
        )
        term = jnp.einsum("is,scj->cij", weights, columns_stack, precision=lax.Precision.HIGHEST)
        return (total + term, None)

    start = jnp.zeros((count, XW, width), jnp.float32)
    total, unused = lax.scan(add_angle, start, (sino, angle_tan))
    return total / sino.shape[0]


def prior(slices, prior_in, prior_out):
    numbers = ("NCHW", "OIHW", "NCHW")
    rounded = slices.astype(jnp.bfloat16)[:, None].astype(jnp.float32)
    hidden = lax.conv_general_dilated(
        rounded, prior_in.astype(jnp.float32), (1, 1), "SAME", dimension_numbers=numbers
    )
    hidden = jnp.maximum(hidden, 0.0).astype(jnp.bfloat16).astype(jnp.float32)
    extra = lax.conv_general_dilated(
        hidden, prior_out.astype(jnp.float32), (1, 1), "SAME", dimension_numbers=numbers
    )
    return slices + extra[:, 0]


def body(
    patches,
    magnitudes,
    probe,
    owners,
    scan_rows,
    scan_cols,
    slab_rows,
    angle_tan,
    prior_in,
    prior_out,
):
    tiles = lax.axis_size("tile")
    angles = lax.axis_size("angle")
    count = patches.shape[1]
    side = patches.shape[3]
    slots = magnitudes.shape[1]
    depth = slots // tiles
    table = dft_table(side)
    owner = owners[0, :, 0]
    member = (owner[:, None] == jnp.arange(tiles, dtype=jnp.int32)[None, :]).astype(jnp.int32)
    before = jnp.sum((jnp.cumsum(member, axis=0) - member) * member, axis=1)
    slot = owner * depth + before
    select = (jnp.arange(slots, dtype=jnp.int32)[:, None] == slot[None, :]).astype(jnp.bfloat16)
    waves = patches[0]
    packed = jnp.dot(select, waves.reshape(count, -1), preferred_element_type=jnp.float32).astype(
        jnp.bfloat16
    )
    arrived = lax.all_to_all(
        packed.reshape(tiles, depth, 2, side, side), "tile", split_axis=0, concat_axis=0, tiled=True
    )
    fixed = correct_all(arrived.reshape(slots, 2, side, side), magnitudes[0], table)
    returned = lax.all_to_all(
        fixed.reshape(tiles, depth, 2, side, side), "tile", split_axis=0, concat_axis=0, tiled=True
    )
    mine = jnp.dot(select.T, returned.reshape(slots, -1), preferred_element_type=jnp.float32)
    mine = mine.astype(jnp.bfloat16).reshape(count, 2, side, side)
    mine_float = mine.astype(jnp.float32)
    contrib = (probe[0] * mine_float[:, 1] - probe[1] * mine_float[:, 0]) * 0.25
    rows_here = scan_rows[0]
    cols_here = scan_cols[0]
    width = W

    def place(step, canvas):
        row = rows_here[step]
        col = cols_here[step]
        piece = lax.dynamic_slice(canvas, (row, col), (side, side)) + contrib[step]
        return lax.dynamic_update_slice(canvas, piece, (row, col))

    canvas = lax.fori_loop(0, count, place, jnp.zeros((H, width), jnp.float32))
    strip = lax.psum_scatter(
        canvas.astype(jnp.bfloat16), "tile", scatter_dimension=0, tiled=True
    ).astype(jnp.float32)
    strip_rows = strip.shape[0]
    rowcap = 2 * strip_rows // angles
    lengths = slab_rows[0]
    starts = jnp.cumsum(lengths) - lengths
    within = jnp.arange(rowcap, dtype=jnp.int32)
    index = jnp.clip(starts[:, None] + within[None, :], 0, strip_rows - 1)
    valid = (within[None, :] < lengths[:, None]).astype(jnp.float32)
    outgoing = strip[index] * valid[:, :, None]
    slabs = prior(
        backproject(
            lax.all_to_all(
                outgoing.astype(jnp.bfloat16), "angle", split_axis=0, concat_axis=0, tiled=True
            ).astype(outgoing.dtype),
            angle_tan,
            width,
        ),
        prior_in,
        prior_out,
    )
    return slabs[None]


def solution(mesh):
    placed = (
        P("angle", "tile", None, None, None),
        P("angle", "tile", None, None),
        P(),
        P("angle", "tile", None),
        P("angle", "tile"),
        P("angle", "tile"),
        P("tile", None),
        P(),
        P(),
        P(),
    )
    return jax.shard_map(
        body, mesh=mesh, in_specs=placed, out_specs=P("tile", "angle", None, None), check_vma=False
    )
```

profile of v0, /device:TPU:1, one launch (start us, length us, event | category | flops | bytes accessed | tf_op | source)
XLA Modules:
  0.0 744.7 jit_solution(15535922218430683627)
XLA Ops:
  11.3 3.1 copy.119
  14.4 14.0 %all-to-all-start = ((bf16[32,2,2,128,128]{4,3,2,1,0:T(8,128)(2,1)}), bf16[32,2,2,128,128]{4,3,2,1,0:T(8,128)(2,1)}, u32[]{:S(2)}, u32[]{:S(2)}) async-start(bf16[32,2,2,128,128]{4,3,2,1,0:T(8,128)(2,1)} %bitcast.193), calls=%async_computation | async-start | bytes 8388608 | tf_op jit(solution)/shard_map/all_to_all | solution.py:121
  29.0 91.9 %all-to-all-done = bf16[32,2,2,128,128]{4,3,2,1,0:T(8,128)(2,1)} async-done(((bf16[32,2,2,128,128]{4,3,2,1,0:T(8,128)(2,1)}), bf16[32,2,2,128,128]{4,3,2,1,0:T(8,128)(2,1)}, u32[]{:S(2)}, u32[]{:S(2)}) %all-to-all-start) | async-done | bytes 4194336 | tf_op jit(solution)/shard_map/all_to_all | solution.py:121
  121.0 2.7 fusion.82
  125.0 2.5 fusion.81
  127.5 4.1 copy.115
  131.6 2.9 copy.116
  134.5 2.9 pad_maximum_fusion
  141.9 6.8 fusion.35
  151.3 2.3 pad_maximum_fusion.1
  153.6 7.0 copy.112
  160.6 3.5 fusion.44
  164.1 2.3 copy.100
  166.4 9.7 %all-to-all-start.1 = ((bf16[32,2,2,128,128]{4,3,2,1,0:T(8,128)(2,1)}), bf16[32,2,2,128,128]{4,3,2,1,0:T(8,128)(2,1)}, u32[]{:S(2)}, u32[]{:S(2)}) async-start(bf16[32,2,2,128,128]{4,3,2,1,0:T(8,128)(2,1)} %copy.100), calls=%async_computation.1 | async-start | bytes 8388608 | tf_op jit(solution)/shard_map/all_to_all | solution.py:125
  176.2 92.5 %all-to-all-done.1 = bf16[32,2,2,128,128]{4,3,2,1,0:T(8,128)(2,1)} async-done(((bf16[32,2,2,128,128]{4,3,2,1,0:T(8,128)(2,1)}), bf16[32,2,2,128,128]{4,3,2,1,0:T(8,128)(2,1)}, u32[]{:S(2)}, u32[]{:S(2)}) %all-to-all-start.1) | async-done | bytes 4194336 | tf_op jit(solution)/shard_map/all_to_all | solution.py:125
  268.7 7.4 reshape.187
  276.1 2.9 convolution_convert_fusion.1
  279.6 60.7 %while.27 = (s32[]{:T(128)}, f32[512,1024]{1,0:T(8,128)S(1)}, s32[8]{0:T(128)S(1)}, s32[8]{0:T(128)S(1)}, f32[8,128,128]{2,1,0:T(8,128)S(1)}, /*index=5*/s32[]{:T(128)}, s32[]{:T(128)}, s32[]{:T(128)}, s32[]{:T(128)}) while((s32[]{:T(128)}, f32[512,1024]{1,0:T(8,128)S(1)}, s32[8]{0:T(128)S(1)}, s32[8]{0:T(128)S(1)}, ...), condition=%wide.region_3.4_spmd, body=%wide.region_2.3_spmd.sunk | while | flops 16392 | bytes 327881 | solution.py:142
  285.2 2.0 dynamic_update_slice.8
  292.8 2.0 dynamic_update_slice.8
  300.4 2.0 dynamic_update_slice.8
  308.1 1.7 dynamic_update_slice.8
  315.3 2.0 dynamic_update_slice.8
  323.0 2.0 dynamic_update_slice.8
  330.6 2.0 dynamic_update_slice.8
  338.3 2.0 dynamic_update_slice.8
  342.0 216.4 %reduce-scatter.2.cloned.1.call-done = bf16[16,1024]{1,0:T(8,128)(2,1)} async-done(((bf16[512,1024]{1,0:T(8,128)(2,1)}), bf16[16,1024]{1,0:T(8,128)(2,1)}) %reduce-scatter.2.cloned.1.call-update) | async-done | bytes 32784 | tf_op jit(solution)/shard_map/reduce_scatter | solution.py:143
  560.6 12.6 %all-to-all-start.2 = ((bf16[16,2,1024]{2,1,0:T(2,128)(2,1)}), bf16[16,2,1024]{2,1,0:T(2,128)(2,1)S(1)}, u32[]{:S(2)}, u32[]{:S(2)}) async-start(bf16[16,2,1024]{2,1,0:T(2,128)(2,1)} %multiply_convert_fusion), calls=%async_computation.3 | async-start | bytes 131072 | tf_op jit(solution)/shard_map/all_to_all | solution.py:156
  573.2 7.8 %all-to-all-done.2 = bf16[16,2,1024]{2,1,0:T(2,128)(2,1)S(1)} async-done(((bf16[16,2,1024]{2,1,0:T(2,128)(2,1)}), bf16[16,2,1024]{2,1,0:T(2,128)(2,1)S(1)}, u32[]{:S(2)}, u32[]{:S(2)}) %all-to-all-start.2) | async-done | bytes 65568 | tf_op jit(solution)/shard_map/all_to_all | solution.py:156
  581.1 46.0 %while.28 = (s32[]{:T(128)}, f32[2,16,1024]{2,1,0:T(8,128)S(1)}, f32[16,2,1024]{2,1,0:T(2,128)S(1)}, f32[16]{0:T(128)S(1)}, s32[]{:T(128)}, /*index=5*/s32[]{:T(128)}) while((s32[]{:T(128)}, f32[2,16,1024]{2,1,0:T(8,128)S(1)}, f32[16,2,1024]{2,1,0:T(2,128)S(1)}, f32[16]{0:T(128)S(1)}, s32[]{:T(128)}, ...), condition=%wide.region_7.8_spmd.clone.clone, body=%wide.region_6.7_spmd.clone.clone.sunk | while | flops 4391977 | bytes 844483 | solution.py:76
  628.9 8.3 %fusion.28 = bf16[16,2,8,129,16]{4,2,1,3,0:T(8,128)(2,1)S(1)} fusion(pred[16,129]{0,1:T(8,128)(4,1)S(1)} %copy-done.9, bf16[1,16,16,131]{2,0,3,1:T(2,128)(2,1)S(1)} %copy.106, bf16[16,1,3,3]{0,3,2,1:T(4,128)(2,1)S(1)} %copy-done), kind=kOutput, calls=%fused_computation.50 | convolution fusion | flops 11228160 | bytes 1126192 | tf_op jit(solution)/shard_map/conv_general_dilated | solution.py:83
  637.3 98.4 %fusion.25 = f32[16,16,129,1]{1,3,2,0:T(1,128)S(1)} fusion(bf16[16,2,7,1,16]{4,2,1,3,0:T(8,128)(2,1)S(1)} %get-tuple-element.258, bf16[16,2,7,1,16]{4,2,1,3,0:T(8,128)(2,1)S(1)} %get-tuple-element.257, bf16[16,2,8,129,16]{4,2,1,3,0:T(8,128)(2,1)S(1)} %fusion.28, bf16[1,16,3,3]{1,3,2,0:T(4,128)(2,1)S(1)} %copy-done.5), kind=kOutput, calls=%fused_computation.48 | convolution fusion | flops 14480384 | bytes 1203488 | tf_op jit(solution)/shard_map/conv_general_dilated | solution.py:87
  (428 shorter events, 76.8 us)
Async XLA Ops:
  6.5 622.3 %copy-start = (bf16[16,1,3,3]{0,3,2,1:T(4,128)(2,1)S(1)}, bf16[16,1,3,3]{0,3,2,1:T(4,128)(2,1)}, u32[]{:S(2)}) copy-start(bf16[16,1,3,3]{0,3,2,1:T(4,128)(2,1)} %param.22) | copy-start | bytes 868
  14.4 106.5 %all-to-all-start = ((bf16[32,2,2,128,128]{4,3,2,1,0:T(8,128)(2,1)}), bf16[32,2,2,128,128]{4,3,2,1,0:T(8,128)(2,1)}, u32[]{:S(2)}, u32[]{:S(2)}) async-start(bf16[32,2,2,128,128]{4,3,2,1,0:T(8,128)(2,1)} %bitcast.193), calls=%async_computation | async-start | bytes 8388608 | tf_op jit(solution)/shard_map/all_to_all | solution.py:121
  140.4 1.6 copy-start.2
  166.4 9.8 %copy-start.3 = (f32[2,128,128]{2,1,0:T(8,128)S(1)}, f32[2,128,128]{2,1,0:T(8,128)}, u32[]{:S(2)}) copy-start(f32[2,128,128]{2,1,0:T(8,128)} %param.16) | copy-start | bytes 393220
  166.4 102.4 %all-to-all-start.1 = ((bf16[32,2,2,128,128]{4,3,2,1,0:T(8,128)(2,1)}), bf16[32,2,2,128,128]{4,3,2,1,0:T(8,128)(2,1)}, u32[]{:S(2)}, u32[]{:S(2)}) async-start(bf16[32,2,2,128,128]{4,3,2,1,0:T(8,128)(2,1)} %copy.100), calls=%async_computation.1 | async-start | bytes 8388608 | tf_op jit(solution)/shard_map/all_to_all | solution.py:125
  176.1 382.3 %reduce-scatter.2.cloned.1.call-start = ((), (), s32[]{:S(2)}) async-start(), calls=%async_computation.4 | async-start | bytes 1081344 | tf_op jit(solution)/shard_map/reduce_scatter | solution.py:143
  276.1 3.5 copy-start.6
  276.1 3.5 copy-start.7
  279.3 62.2 %copy-start.4 = (s32[1,16]{1,0:T(1,128)S(1)}, s32[1,16]{1,0:T(1,128)}, u32[]{:S(2)}) copy-start(s32[1,16]{1,0:T(1,128)} %param.20) | copy-start | bytes 196
  279.6 301.5 %copy-start.8 = (f32[16]{0:T(128)S(1)}, f32[16]{0:T(128)}, u32[]{:S(2)}) copy-start(f32[16]{0:T(128)} %param.21) | copy-start | bytes 196
  559.8 69.1 %copy-start.9 = (pred[16,129]{0,1:T(8,128)(4,1)S(1)}, pred[16,129]{0,1:T(8,128)(4,1)}, u32[]{:S(2)}) copy-start(pred[16,129]{0,1:T(8,128)(4,1)} %constant.130) | copy-start | bytes 6196
  560.6 20.4 %all-to-all-start.2 = ((bf16[16,2,1024]{2,1,0:T(2,128)(2,1)}), bf16[16,2,1024]{2,1,0:T(2,128)(2,1)S(1)}, u32[]{:S(2)}, u32[]{:S(2)}) async-start(bf16[16,2,1024]{2,1,0:T(2,128)(2,1)} %multiply_convert_fusion), calls=%async_computation.3 | async-start | bytes 131072 | tf_op jit(solution)/shard_map/all_to_all | solution.py:156
  628.8 8.4 %copy-start.5 = (bf16[1,16,3,3]{1,3,2,0:T(4,128)(2,1)S(1)}, bf16[1,16,3,3]{1,3,2,0:T(4,128)(2,1)}, u32[]{:S(2)}) copy-start(bf16[1,16,3,3]{1,3,2,0:T(4,128)(2,1)} %param.23) | copy-start | bytes 868
  637.2 100.4 %copy-start.1 = (bf16[16,1,3,3]{0,3,2,1:T(4,128)(2,1)S(1)}, bf16[16,1,3,3]{0,3,2,1:T(4,128)(2,1)}, u32[]{:S(2)}) copy-start(bf16[16,1,3,3]{0,3,2,1:T(4,128)(2,1)} %param.22) | copy-start | bytes 868
Sparse Core Ops, SparseCore 0:
  341.6 216.7 reduce-scatter.1
where the time goes:
time: 749 us; the launch traced here: 745 us
  waiting for transfers between devices  409 us (55%)
  matrix products  123 us (16%)
  local copies, waits for them, and re-layouts  86.2 us (12%)
  other arithmetic  40.3 us (5%)
  starting transfers between devices  36.4 us (5%)
  loops' own time  35.7 us (5%)
  between operations  14 us (2%)
    reduce_scatter x1, waiting for transfers between devices, body(): lax.psum_scatter(canvas.astype(jnp.bfloat16), 'tile', scatter_dimension=0...  216 us
    conv_general_dilated x1, matrix products, prior(): lax.conv_general_dilated(hidden, prior_out.astype(jnp.float32), (1, 1), '...  98.4 us
    all_to_all x1, waiting for transfers between devices, body(): lax.all_to_all(fixed.reshape(tiles, depth, 2, side, side), 'tile', split_...  92.5 us
    all_to_all x1, waiting for transfers between devices, body(): lax.all_to_all(packed.reshape(tiles, depth, 2, side, side), 'tile', split...  91.9 us
    another operation x1, loops' own time, body(): canvas = lax.fori_loop(0, count, place, jnp.zeros((H, width), jnp.float32))  33.3 us
    dynamic_update_slice x8, local copies, waits for them, and re-layouts, place(): return lax.dynamic_update_slice(canvas, piece, (row, col))  16 us
  transfers between devices with their start and end apart: 4, of which 4 were waited for; matrix products, arithmetic and copies ran while one was open for 0% of the time, Pallas kernels for 0%

commit v1 on v0

--- a/solution.py
+++ b/solution.py
@@ -1,3 +1,4 @@
+import functools
 import math
 import jax
 import jax.numpy as jnp
@@ -7,6 +8,25 @@
 H = 512
 W = 1024
 XW = 16
+
+
+def meet_joints(here_x, lane_axis, array_dim, dim_at):
+    block_now, r1 = (lax.axis_size(lane_axis), lax.axis_index(lane_axis))
+    block_next = here_x.shape[array_dim] // block_now
+    mat_out = list(here_x.shape)
+    mat_out[array_dim] = block_next
+    u1 = mat_out[dim_at]
+    mat_out[dim_at] = u1 * block_now
+    new = jnp.zeros(mat_out, here_x.dtype)
+    for j in range(block_now):
+        z1 = lax.dynamic_slice_in_dim(here_x, (r1 ^ j) * block_next, block_next, axis=array_dim)
+        if j:
+            z1 = lax.ppermute(z1, lane_axis, list(map(lambda ix: (ix, ix ^ j), range(block_now))))
+        new = lax.dynamic_update_slice_in_dim(new, z1, (r1 ^ j) * u1, axis=dim_at)
+    return new
+
+
+match_the_scales = functools.partial(meet_joints, lane_axis="angle", array_dim=0, dim_at=0)
 
 
 def dft_table(side):
@@ -153,11 +173,7 @@
     outgoing = strip[index] * valid[:, :, None]
     slabs = prior(
         backproject(
-            lax.all_to_all(
-                outgoing.astype(jnp.bfloat16), "angle", split_axis=0, concat_axis=0, tiled=True
-            ).astype(outgoing.dtype),
-            angle_tan,
-            width,
+            match_the_scales(outgoing.astype(jnp.bfloat16)).astype(outgoing.dtype), angle_tan, width
         ),
         prior_in,
         prior_out,

time: 749 us -> 797 us (1.064)
  starting transfers between devices: 36.4 us -> 83.3 us
  matrix products: 123 us -> 139 us
    ppermute x0 -> x15, starting transfers between devices: none -> 59.5 us  [meet_joints(): lax.ppermute(z1, lane_axis, list(map(lambda ix: (ix, ix ^ j), range(block...]
    conv_general_dilated x1, matrix products: 98.4 us -> 114 us  [prior(): lax.conv_general_dilated(hidden, prior_out.astype(jnp.float32), (1, 1), '...]
    all_to_all x1 -> x0, starting transfers between devices: 12.6 us -> none  [body(): lax.all_to_all(outgoing.astype(jnp.bfloat16), 'angle', split_axis=0, conc...]
  transfers between devices with their start and end apart: 4 -> 18, of which waited for: 4 -> 4; matrix products, arithmetic and copies ran while one was open for 0% -> 0% of each run, Pallas kernels for 0% -> 0%
where the time goes in v1:
time: 797 us; the launch traced here: 793 us
  waiting for transfers between devices  404 us (51%)
  matrix products  139 us (17%)
  local copies, waits for them, and re-layouts  86.1 us (11%)
  starting transfers between devices  83.3 us (10%)
  other arithmetic  36.9 us (5%)
  loops' own time  29.9 us (4%)
  between operations  14.5 us (2%)
    reduce_scatter x1, waiting for transfers between devices, body(): lax.psum_scatter(canvas.astype(jnp.bfloat16), 'tile', scatter_dimension=0...  216 us
    conv_general_dilated x1, matrix products, prior(): lax.conv_general_dilated(hidden, prior_out.astype(jnp.float32), (1, 1), '...  114 us
    all_to_all x1, waiting for transfers between devices, body(): lax.all_to_all(fixed.reshape(tiles, depth, 2, side, side), 'tile', split_...  92.6 us
    all_to_all x1, waiting for transfers between devices, body(): lax.all_to_all(packed.reshape(tiles, depth, 2, side, side), 'tile', split...  91.9 us
    ppermute x15, starting transfers between devices, meet_joints(): lax.ppermute(z1, lane_axis, list(map(lambda ix: (ix, ix ^ j), range(block...  59.5 us
    another operation x1, loops' own time, body(): canvas = lax.fori_loop(0, count, place, jnp.zeros((H, width), jnp.float32))  27.6 us
    dynamic_update_slice x8, local copies, waits for them, and re-layouts, place(): return lax.dynamic_update_slice(canvas, piece, (row, col))  16 us
  transfers between devices with their start and end apart: 18, of which 4 were waited for; matrix products, arithmetic and copies ran while one was open for 0% of the time, Pallas kernels for 0%

profile of v1, /device:TPU:1, one launch (start us, length us, event | category | flops | bytes accessed | tf_op | source)
XLA Modules:
  0.0 793.1 jit_solution(14614881016908329928)
XLA Ops:
  11.3 3.2 copy.118
  14.5 14.0 %all-to-all-start = ((bf16[32,2,2,128,128]{4,3,2,1,0:T(8,128)(2,1)}), bf16[32,2,2,128,128]{4,3,2,1,0:T(8,128)(2,1)}, u32[]{:S(2)}, u32[]{:S(2)}) async-start(bf16[32,2,2,128,128]{4,3,2,1,0:T(8,128)(2,1)} %bitcast.193), calls=%async_computation | async-start | bytes 8388608 | tf_op jit(solution)/shard_map/all_to_all | solution.py:141
  29.1 91.9 %all-to-all-done = bf16[32,2,2,128,128]{4,3,2,1,0:T(8,128)(2,1)} async-done(((bf16[32,2,2,128,128]{4,3,2,1,0:T(8,128)(2,1)}), bf16[32,2,2,128,128]{4,3,2,1,0:T(8,128)(2,1)}, u32[]{:S(2)}, u32[]{:S(2)}) %all-to-all-start) | async-done | bytes 4194336 | tf_op jit(solution)/shard_map/all_to_all | solution.py:141
  121.0 2.7 fusion.82
  125.0 2.5 fusion.81
  127.5 4.1 copy.114
  131.6 2.9 copy.115
  134.5 2.9 pad_maximum_fusion
  141.9 6.7 fusion.35
  153.5 7.0 copy.112
  160.5 3.5 fusion.44
  166.3 9.7 %all-to-all-start.1 = ((bf16[32,2,2,128,128]{4,3,2,1,0:T(8,128)(2,1)}), bf16[32,2,2,128,128]{4,3,2,1,0:T(8,128)(2,1)}, u32[]{:S(2)}, u32[]{:S(2)}) async-start(bf16[32,2,2,128,128]{4,3,2,1,0:T(8,128)(2,1)} %copy.100), calls=%async_computation.1 | async-start | bytes 8388608 | tf_op jit(solution)/shard_map/all_to_all | solution.py:145
  176.1 92.6 %all-to-all-done.1 = bf16[32,2,2,128,128]{4,3,2,1,0:T(8,128)(2,1)} async-done(((bf16[32,2,2,128,128]{4,3,2,1,0:T(8,128)(2,1)}), bf16[32,2,2,128,128]{4,3,2,1,0:T(8,128)(2,1)}, u32[]{:S(2)}, u32[]{:S(2)}) %all-to-all-start.1) | async-done | bytes 4194336 | tf_op jit(solution)/shard_map/all_to_all | solution.py:145
  268.7 7.3 reshape.187
  276.1 2.9 convolution_convert_fusion.1
  279.6 53.6 %while.27 = (s32[]{:T(128)}, f32[512,1024]{1,0:T(8,128)S(1)}, s32[8]{0:T(128)S(1)}, s32[8]{0:T(128)S(1)}, f32[8,128,128]{2,1,0:T(8,128)S(1)}, /*index=5*/s32[]{:T(128)}, s32[]{:T(128)}, s32[]{:T(128)}, s32[]{:T(128)}) while((s32[]{:T(128)}, f32[512,1024]{1,0:T(8,128)S(1)}, s32[8]{0:T(128)S(1)}, s32[8]{0:T(128)S(1)}, ...), condition=%wide.region_3.4_spmd, body=%wide.region_2.3_spmd.sunk | while | flops 16392 | bytes 327881 | solution.py:162
  335.0 216.3 %reduce-scatter.2.cloned.1.call-done = bf16[16,1024]{1,0:T(8,128)(2,1)} async-done(((bf16[512,1024]{1,0:T(8,128)(2,1)}), bf16[16,1024]{1,0:T(8,128)(2,1)}) %reduce-scatter.2.cloned.1.call-update) | async-done | bytes 32784 | tf_op jit(solution)/shard_map/reduce_scatter | solution.py:163
  553.0 7.8 collective-permute-start
  560.8 3.2 collective-permute-start.1
  566.3 4.1 collective-permute-start.3
  570.4 2.5 collective-permute-start.4
  572.9 5.0 collective-permute-start.5
  580.2 7.2 collective-permute-start.7
  589.8 4.5 collective-permute-start.9
  594.3 4.0 collective-permute-start.10
  598.3 3.6 collective-permute-start.11
  601.9 4.2 collective-permute-start.12
  606.1 4.6 collective-permute-start.13
  614.2 2.7 collective-permute-done.14
  617.0 43.0 %while.28 = (s32[]{:T(128)}, f32[2,16,1024]{2,1,0:T(8,128)S(1)}, f32[16,2,1024]{2,0,1:T(8,128)S(1)}, f32[16]{0:T(128)S(1)}, s32[]{:T(128)}, /*index=5*/s32[]{:T(128)}) while((s32[]{:T(128)}, f32[2,16,1024]{2,1,0:T(8,128)S(1)}, f32[16,2,1024]{2,0,1:T(8,128)S(1)}, f32[16]{0:T(128)S(1)}, s32[]{:T(128)}, ...), condition=%wide.region_7.8_spmd.clone.clone, body=%wide.region_6.7_spmd.clone.clone.sunk | while | flops 4391977 | bytes 828095 | solution.py:96
  661.8 8.3 %fusion.28 = bf16[16,2,8,129,16]{4,2,1,3,0:T(8,128)(2,1)S(1)} fusion(pred[16,129]{0,1:T(8,128)(4,1)S(1)} %copy-done.9, bf16[1,16,16,131]{2,0,3,1:T(2,128)(2,1)S(1)} %copy.106, bf16[16,1,3,3]{0,3,2,1:T(4,128)(2,1)S(1)} %copy-done), kind=kOutput, calls=%fused_computation.51 | convolution fusion | flops 11228160 | bytes 1126192 | tf_op jit(solution)/shard_map/conv_general_dilated | solution.py:103
  670.2 113.9 %fusion.25 = f32[16,16,129,1]{1,3,2,0:T(1,128)S(1)} fusion(bf16[16,2,7,1,16]{4,2,1,3,0:T(8,128)(2,1)S(1)} %get-tuple-element.250, bf16[16,2,7,1,16]{4,2,1,3,0:T(8,128)(2,1)S(1)} %get-tuple-element.249, bf16[16,2,8,129,16]{4,2,1,3,0:T(8,128)(2,1)S(1)} %fusion.28, bf16[1,16,3,3]{1,3,2,0:T(4,128)(2,1)S(1)} %copy-done.5), kind=kOutput, calls=%fused_computation.49 | convolution fusion | flops 14480384 | bytes 1203488 | tf_op jit(solution)/shard_map/conv_general_dilated | solution.py:107
  (458 shorter events, 103.1 us)
Async XLA Ops:
  6.5 655.3 %copy-start = (bf16[16,1,3,3]{0,3,2,1:T(4,128)(2,1)S(1)}, bf16[16,1,3,3]{0,3,2,1:T(4,128)(2,1)}, u32[]{:S(2)}) copy-start(bf16[16,1,3,3]{0,3,2,1:T(4,128)(2,1)} %param.22) | copy-start | bytes 868
  14.5 106.5 %all-to-all-start = ((bf16[32,2,2,128,128]{4,3,2,1,0:T(8,128)(2,1)}), bf16[32,2,2,128,128]{4,3,2,1,0:T(8,128)(2,1)}, u32[]{:S(2)}, u32[]{:S(2)}) async-start(bf16[32,2,2,128,128]{4,3,2,1,0:T(8,128)(2,1)} %bitcast.193), calls=%async_computation | async-start | bytes 8388608 | tf_op jit(solution)/shard_map/all_to_all | solution.py:141
  140.4 1.6 copy-start.2
  166.3 9.8 %copy-start.3 = (f32[2,128,128]{2,1,0:T(8,128)S(1)}, f32[2,128,128]{2,1,0:T(8,128)}, u32[]{:S(2)}) copy-start(f32[2,128,128]{2,1,0:T(8,128)} %param.16) | copy-start | bytes 393220
  166.3 102.4 %all-to-all-start.1 = ((bf16[32,2,2,128,128]{4,3,2,1,0:T(8,128)(2,1)}), bf16[32,2,2,128,128]{4,3,2,1,0:T(8,128)(2,1)}, u32[]{:S(2)}, u32[]{:S(2)}) async-start(bf16[32,2,2,128,128]{4,3,2,1,0:T(8,128)(2,1)} %copy.100), calls=%async_computation.1 | async-start | bytes 8388608 | tf_op jit(solution)/shard_map/all_to_all | solution.py:145
  176.1 375.2 %reduce-scatter.2.cloned.1.call-start = ((), (), s32[]{:S(2)}) async-start(), calls=%async_computation.3 | async-start | bytes 1081344 | tf_op jit(solution)/shard_map/reduce_scatter | solution.py:163
  276.1 3.5 copy-start.6
  276.1 3.5 copy-start.7
  279.3 55.1 %copy-start.4 = (s32[1,16]{1,0:T(1,128)S(1)}, s32[1,16]{1,0:T(1,128)}, u32[]{:S(2)}) copy-start(s32[1,16]{1,0:T(1,128)} %param.20) | copy-start | bytes 196
  279.6 337.4 %copy-start.8 = (f32[16]{0:T(128)S(1)}, f32[16]{0:T(128)}, u32[]{:S(2)}) copy-start(f32[16]{0:T(128)} %param.21) | copy-start | bytes 196
  552.6 109.2 %copy-start.9 = (pred[16,129]{0,1:T(8,128)(4,1)S(1)}, pred[16,129]{0,1:T(8,128)(4,1)}, u32[]{:S(2)}) copy-start(pred[16,129]{0,1:T(8,128)(4,1)} %constant.166) | copy-start | bytes 6196
  553.0 19.8 %collective-permute-start = (bf16[1,2,1024]{2,0,1:T(2,128)(2,1)S(1)}, bf16[1,2,1024]{2,0,1:T(2,128)(2,1)S(1)}, u32[]{:S(2)}, u32[]{:S(2)}) collective-permute-start(bf16[1,2,1024]{2,0,1:T(2,128)(2,1)S(1)} %get-tuple-element.277), channel_id=1, source_target_pairs={{0,32},{32,0},{64,96},{96,64},{128,160},{160,128},{192,224},{224,1... | collective-permute-start | bytes 12296 | tf_op jit(solution)/shard_map/ppermute | solution.py:24
  560.8 17.0 %collective-permute-start.1 = (bf16[1,2,1024]{2,0,1:T(2,128)(2,1)S(1)}, bf16[1,2,1024]{2,0,1:T(2,128)(2,1)S(1)}, u32[]{:S(2)}, u32[]{:S(2)}) collective-permute-start(bf16[1,2,1024]{2,0,1:T(2,128)(2,1)S(1)} %get-tuple-element.276), channel_id=1, source_target_pairs={{0,64},{32,96},{64,0},{96,32},{128,192},{160,224},{192,128},{224,1... | collective-permute-start | bytes 12296 | tf_op jit(solution)/shard_map/ppermute | solution.py:24
  564.0 16.2 %collective-permute-start.2 = (bf16[1,2,1024]{2,0,1:T(2,128)(2,1)S(1)}, bf16[1,2,1024]{2,0,1:T(2,128)(2,1)S(1)}, u32[]{:S(2)}, u32[]{:S(2)}) collective-permute-start(bf16[1,2,1024]{2,0,1:T(2,128)(2,1)S(1)} %get-tuple-element.275), channel_id=1, source_target_pairs={{0,96},{32,64},{64,32},{96,0},{128,224},{160,192},{192,160},{224,1... | collective-permute-start | bytes 12296 | tf_op jit(solution)/shard_map/ppermute | solution.py:24
  566.3 21.1 %collective-permute-start.3 = (bf16[1,2,1024]{2,0,1:T(2,128)(2,1)S(1)}, bf16[1,2,1024]{2,0,1:T(2,128)(2,1)S(1)}, u32[]{:S(2)}, u32[]{:S(2)}) collective-permute-start(bf16[1,2,1024]{2,0,1:T(2,128)(2,1)S(1)} %get-tuple-element.274), channel_id=1, source_target_pairs={{0,128},{32,160},{64,192},{96,224},{128,0},{160,32},{192,64},{224,... | collective-permute-start | bytes 12296 | tf_op jit(solution)/shard_map/ppermute | solution.py:24
  570.4 19.4 %collective-permute-start.4 = (bf16[1,2,1024]{2,0,1:T(2,128)(2,1)S(1)}, bf16[1,2,1024]{2,0,1:T(2,128)(2,1)S(1)}, u32[]{:S(2)}, u32[]{:S(2)}) collective-permute-start(bf16[1,2,1024]{2,0,1:T(2,128)(2,1)S(1)} %get-tuple-element.273), channel_id=1, source_target_pairs={{0,160},{32,128},{64,224},{96,192},{128,32},{160,0},{192,96},{224,... | collective-permute-start | bytes 12296 | tf_op jit(solution)/shard_map/ppermute | solution.py:24
  572.9 21.4 %collective-permute-start.5 = (bf16[1,2,1024]{2,0,1:T(2,128)(2,1)S(1)}, bf16[1,2,1024]{2,0,1:T(2,128)(2,1)S(1)}, u32[]{:S(2)}, u32[]{:S(2)}) collective-permute-start(bf16[1,2,1024]{2,0,1:T(2,128)(2,1)S(1)} %get-tuple-element.272), channel_id=1, source_target_pairs={{0,192},{32,224},{64,128},{96,160},{128,64},{160,96},{192,0},{224,... | collective-permute-start | bytes 12296 | tf_op jit(solution)/shard_map/ppermute | solution.py:24
  577.9 20.4 %collective-permute-start.6 = (bf16[1,2,1024]{2,0,1:T(2,128)(2,1)S(1)}, bf16[1,2,1024]{2,0,1:T(2,128)(2,1)S(1)}, u32[]{:S(2)}, u32[]{:S(2)}) collective-permute-start(bf16[1,2,1024]{2,0,1:T(2,128)(2,1)S(1)} %get-tuple-element.271), channel_id=1, source_target_pairs={{0,224},{32,192},{64,160},{96,128},{128,96},{160,64},{192,32},{224... | collective-permute-start | bytes 12296 | tf_op jit(solution)/shard_map/ppermute | solution.py:24
  580.2 21.7 %collective-permute-start.7 = (bf16[1,2,1024]{2,0,1:T(2,128)(2,1)S(1)}, bf16[1,2,1024]{2,0,1:T(2,128)(2,1)S(1)}, u32[]{:S(2)}, u32[]{:S(2)}) collective-permute-start(bf16[1,2,1024]{2,0,1:T(2,128)(2,1)S(1)} %get-tuple-element.270), channel_id=1, source_target_pairs={{0,256},{32,288},{64,320},{96,352},{128,384},{160,416},{192,448},{... | collective-permute-start | bytes 12296 | tf_op jit(solution)/shard_map/ppermute | solution.py:24
  587.3 18.7 %collective-permute-start.8 = (bf16[1,2,1024]{2,0,1:T(2,128)(2,1)S(1)}, bf16[1,2,1024]{2,0,1:T(2,128)(2,1)S(1)}, u32[]{:S(2)}, u32[]{:S(2)}) collective-permute-start(bf16[1,2,1024]{2,0,1:T(2,128)(2,1)S(1)} %get-tuple-element.269), channel_id=1, source_target_pairs={{0,288},{32,256},{64,352},{96,320},{128,416},{160,384},{192,480},{... | collective-permute-start | bytes 12296 | tf_op jit(solution)/shard_map/ppermute | solution.py:24
  589.8 20.9 %collective-permute-start.9 = (bf16[1,2,1024]{2,0,1:T(2,128)(2,1)S(1)}, bf16[1,2,1024]{2,0,1:T(2,128)(2,1)S(1)}, u32[]{:S(2)}, u32[]{:S(2)}) collective-permute-start(bf16[1,2,1024]{2,0,1:T(2,128)(2,1)S(1)} %get-tuple-element.268), channel_id=1, source_target_pairs={{0,320},{32,352},{64,256},{96,288},{128,448},{160,480},{192,384},{... | collective-permute-start | bytes 12296 | tf_op jit(solution)/shard_map/ppermute | solution.py:24
  594.3 19.5 %collective-permute-start.10 = (bf16[1,2,1024]{2,0,1:T(2,128)(2,1)S(1)}, bf16[1,2,1024]{2,0,1:T(2,128)(2,1)S(1)}, u32[]{:S(2)}, u32[]{:S(2)}) collective-permute-start(bf16[1,2,1024]{2,0,1:T(2,128)(2,1)S(1)} %get-tuple-element.267), channel_id=1, source_target_pairs={{0,352},{32,320},{64,288},{96,256},{128,480},{160,448},{192,416},{... | collective-permute-start | bytes 12296 | tf_op jit(solution)/shard_map/ppermute | solution.py:24
  598.3 15.6 %collective-permute-start.11 = (bf16[1,2,1024]{2,0,1:T(2,128)(2,1)S(1)}, bf16[1,2,1024]{2,0,1:T(2,128)(2,1)S(1)}, u32[]{:S(2)}, u32[]{:S(2)}) collective-permute-start(bf16[1,2,1024]{2,0,1:T(2,128)(2,1)S(1)} %get-tuple-element.266), channel_id=1, source_target_pairs={{0,384},{32,416},{64,448},{96,480},{128,256},{160,288},{192,320},{... | collective-permute-start | bytes 12296 | tf_op jit(solution)/shard_map/ppermute | solution.py:24
  601.9 12.1 %collective-permute-start.12 = (bf16[1,2,1024]{2,0,1:T(2,128)(2,1)S(1)}, bf16[1,2,1024]{2,0,1:T(2,128)(2,1)S(1)}, u32[]{:S(2)}, u32[]{:S(2)}) collective-permute-start(bf16[1,2,1024]{2,0,1:T(2,128)(2,1)S(1)} %get-tuple-element.265), channel_id=1, source_target_pairs={{0,416},{32,384},{64,480},{96,448},{128,288},{160,256},{192,352},{... | collective-permute-start | bytes 12296 | tf_op jit(solution)/shard_map/ppermute | solution.py:24
  606.1 8.0 %collective-permute-start.13 = (bf16[1,2,1024]{2,0,1:T(2,128)(2,1)S(1)}, bf16[1,2,1024]{2,0,1:T(2,128)(2,1)S(1)}, u32[]{:S(2)}, u32[]{:S(2)}) collective-permute-start(bf16[1,2,1024]{2,0,1:T(2,128)(2,1)S(1)} %get-tuple-element.264), channel_id=1, source_target_pairs={{0,448},{32,480},{64,384},{96,416},{128,320},{160,352},{192,256},{... | collective-permute-start | bytes 12296 | tf_op jit(solution)/shard_map/ppermute | solution.py:24
  610.7 6.2 collective-permute-start.14
  661.8 8.4 %copy-start.5 = (bf16[1,16,3,3]{1,3,2,0:T(4,128)(2,1)S(1)}, bf16[1,16,3,3]{1,3,2,0:T(4,128)(2,1)}, u32[]{:S(2)}) copy-start(bf16[1,16,3,3]{1,3,2,0:T(4,128)(2,1)} %param.23) | copy-start | bytes 868
  670.2 115.9 %copy-start.1 = (bf16[16,1,3,3]{0,3,2,1:T(4,128)(2,1)S(1)}, bf16[16,1,3,3]{0,3,2,1:T(4,128)(2,1)}, u32[]{:S(2)}) copy-start(bf16[16,1,3,3]{0,3,2,1:T(4,128)(2,1)} %param.22) | copy-start | bytes 868
Sparse Core Ops, SparseCore 0:
  334.5 216.7 reduce-scatter.1
